TPU v7x, 32 devices: a whole 2x2x4 slice. The times are simulated.
32 devices in a mesh: mem: 2 (over x), reg: 16 (over z, y, core).
Axes of the slice: x: 2, y: 2, z: 4, core: 2. Of those that a mesh axis runs over, the one named last changes fastest.
Arguments:
- members: bfloat16 [512, 256, 128], P('mem', 'reg'), may hold values from -6 to 6
- diffusivity: float32 [256, 128], P('reg'), may hold values from 0.02 to 0.2
- advection: float32 [256, 128], P('reg'), may hold values from -0.3 to 0.3
- obs_value: bfloat16 [16, 2, 256], P('reg', 'mem'), may hold values from -6 to 6
- obs_rinv: float32 [16, 2, 256], P('reg', 'mem'), may hold values from 0.5 to 4
- obs_cell: int32 [16, 2, 256], P('reg', 'mem'), may hold values from 0 to 1023
- obs_count: int32 [16, 2], P('reg', 'mem'), may hold values from 64 to 256, as said below
- loc_index: int32 [16, 2, 256], P('reg', 'mem'), may hold values from 0 to 7
Outputs:
- analysis: float32 [512, 256, 128], P('mem', 'reg')
Inputs may be any that keep to these rules, and one draw needn't show every extreme that they name: `obs_count`: each patch has 64 to 256 live slots, and some patch has exactly 256.
All inputs are finite; a program needn't handle non-finite values.
Results may differ from a plain program's by a relative error of at most 0.0047.
Values may be sent and summed in bfloat16 or wider, within the bound.
A program may use at most 64 MiB of HBM per device.

v0:
```python
import jax
import jax.numpy as jnp
from jax import lax
from jax.sharding import PartitionSpec as P

STEPS = 3
NSIT = 2


def with_halo(cells, sides, width):
    for axis, dim in sides:
        count = lax.axis_size(axis)
        head = lax.slice_in_dim(cells, 0, width, axis=dim)
        tail = lax.slice_in_dim(cells, cells.shape[dim] - width, cells.shape[dim], axis=dim)
        cells = jnp.concatenate(
            [
                lax.ppermute(tail, axis, [(i, (i + 1) % count) for i in range(count)]),
                cells,
                lax.ppermute(head, axis, [((i + 1) % count, i) for i in range(count)]),
            ],
            axis=dim,
        )
    return cells


def advance(padded, diffusion, advect):
    centre = padded[:, 1:-1]
    north_row = padded[:, :-2]
    south_row = padded[:, 2:]
    east_cell = jnp.roll(centre, -1, 2)
    west_cell = jnp.roll(centre, 1, 2)
    return (
        centre
        + diffusion * (north_row + south_row + east_cell + west_cell - 4.0 * centre)
        - advect * 0.5 * (south_row - north_row)
    )


def analyse(states, ens_obs, value_all, prec_all):
    members_count = states.shape[0]
    identity = jnp.eye(members_count, dtype=jnp.float32)
    obs_float = ens_obs.astype(jnp.float32)
    obs_mean = jnp.mean(obs_float, axis=0)
    obs_perturb = obs_float - obs_mean[None, :]
    innovation = value_all - obs_mean
    weighted = obs_perturb * prec_all[None, :]
    system = (
        jnp.dot(weighted, obs_perturb.T, precision=lax.Precision.HIGHEST)
        + (members_count - 1.0) * identity
    )
    forcing = jnp.dot(weighted, innovation, precision=lax.Precision.HIGHEST)
    scale_value = jnp.sqrt(jnp.sum(system * system))
    root_iter = system / scale_value
    inverse_root = identity
    for sweep in range(NSIT):
        correction = 1.5 * identity - 0.5 * jnp.dot(
            inverse_root, root_iter, precision=lax.Precision.HIGHEST
        )
        root_iter = jnp.dot(root_iter, correction, precision=lax.Precision.HIGHEST)
        inverse_root = jnp.dot(correction, inverse_root, precision=lax.Precision.HIGHEST)
    mean_weights = (
        jnp.dot(
            inverse_root,
            jnp.dot(inverse_root, forcing, precision=lax.Precision.HIGHEST),
            precision=lax.Precision.HIGHEST,
        )
        / scale_value
    )
    transform = (
        jnp.sqrt((members_count - 1.0) / scale_value) * inverse_root + mean_weights[:, None]
    ).astype(jnp.bfloat16)
    state_float = states.astype(jnp.float32)
    state_mean = jnp.mean(state_float, axis=0)
    state_perturb = (state_float - state_mean[None, :]).astype(jnp.bfloat16)
    return state_mean[None, :] + jnp.dot(
        transform.T, state_perturb, preferred_element_type=jnp.float32
    )


def on_device(members, diffusivity, advection, obs_value, obs_rinv, obs_cell, obs_count, loc_index):
    ensemble_sample_array = members.astype(jnp.float32)
    padded = with_halo(ensemble_sample_array.astype(jnp.bfloat16), (("reg", 1),), STEPS).astype(
        ensemble_sample_array.dtype
    )
    coefficients = with_halo(jnp.stack([diffusivity, advection]), (("reg", 1),), STEPS)
    total_rows = coefficients.shape[1]
    for level_index in range(STEPS):
        inner_rows = coefficients[:, level_index + 1 : total_rows - level_index - 1]
        padded = advance(padded, inner_rows[0], inner_rows[1])
    ensemble_sample_array = padded
    propagate_ensemble = ensemble_sample_array.astype(jnp.bfloat16)
    zone_ensemble, lines_in_zone, lattice_breadth = propagate_ensemble.shape
    grouped_members = lax.axis_size("mem")
    rows_per_patch = lines_in_zone // grouped_members
    refolded_values = propagate_ensemble.reshape(
        zone_ensemble, grouped_members, rows_per_patch * lattice_breadth
    )
    owned = lax.all_to_all(refolded_values, "mem", split_axis=1, concat_axis=0, tiled=True)
    states = owned[:, 0]
    obs_cells = obs_cell[0, 0]
    obs_space = jnp.take(states, obs_cells, axis=1)
    slot_index = jnp.arange(obs_cells.shape[0], dtype=jnp.int32)
    live_slot = (slot_index < obs_count[0, 0]).astype(jnp.float32)
    own_prec = obs_rinv[0, 0] * live_slot
    loc_float = loc_index[0, 0].astype(jnp.float32)
    far_prec = (own_prec * jnp.exp(-(((loc_float + 1.0) / 4.0) ** 2))).astype(jnp.bfloat16)
    obs_info = jnp.stack([obs_value[0, 0], far_prec])
    space_pad, info_pad = (
        with_halo(obs_space[None], (("reg", 0),), 1),
        with_halo(obs_info[None], (("reg", 0),), 1),
    )
    ens_obs = jnp.concatenate([obs_space, space_pad[0], space_pad[2]], axis=1)
    value_all = jnp.concatenate([obs_value[0, 0], info_pad[0, 0], info_pad[2, 0]]).astype(
        jnp.float32
    )
    prec_all = jnp.concatenate(
        [own_prec, info_pad[0, 1].astype(jnp.float32), info_pad[2, 1].astype(jnp.float32)]
    )
    analysed = analyse(states, ens_obs, value_all, prec_all)
    shaped_back = analysed.reshape(analysed.shape[0], rows_per_patch, lattice_breadth)
    returned = lax.all_to_all(shaped_back, "mem", split_axis=0, concat_axis=1, tiled=True)
    return returned


def solution(mesh):
    return jax.shard_map(
        on_device,
        mesh=mesh,
        in_specs=(
            P("mem", "reg", None),
            P("reg", None),
            P("reg", None),
            P("reg", "mem", None),
            P("reg", "mem", None),
            P("reg", "mem", None),
            P("reg", "mem"),
            P("reg", "mem", None),
        ),
        out_specs=P("mem", "reg", None),
        check_vma=False,
    )
```

profile of v0, /device:TPU:0, one launch (start us, length us, event | category | flops | bytes accessed | tf_op | source)
XLA Modules:
  0.0 114.7 jit_solution(7514765113728840027)
XLA Ops:
  2.5 5.1 %collective-permute-start.7 = (bf16[1,2,256]{2,1,0:T(2,128)(2,1)S(1)}, bf16[1,2,256]{2,1,0:T(2,128)(2,1)S(1)}, u32[]{:S(2)}, u32[]{:S(2)}) collective-permute-start(bf16[1,2,256]{2,1,0:T(2,128)(2,1)S(1)} %maximum_bitcast_fusion), channel_id=1, source_target_pairs={{1,0},{2,1},{3,2},{4,3},{5,4},{6,5},{7,6},{8,7},{9,8},{10,9},{11,1... | collective-permute-start | bytes 3080 | tf_op jit(solution)/shard_map/ppermute | solution.py:19
  8.3 4.4 %collective-permute-start.3 = (f32[2,3,128]{2,1,0:T(4,128)S(1)}, f32[2,3,128]{2,1,0:T(4,128)S(1)}, u32[]{:S(2)}, u32[]{:S(2)}) collective-permute-start(f32[2,3,128]{2,1,0:T(4,128)S(1)} %get-tuple-element.24), channel_id=1, source_target_pairs={{1,0},{2,1},{3,2},{4,3},{5,4},{6,5},{7,6},{8,7},{9,8},{10,9},{11,1... | collective-permute-start | bytes 9224 | tf_op jit(solution)/shard_map/ppermute | solution.py:19
  12.7 1.4 %fusion.45 = (bf16[256,3,128]{2,1,0:T(4,128)(2,1)S(1)}, bf16[256,3,128]{2,1,0:T(4,128)(2,1)S(1)}) fusion(bf16[256,16,128]{2,1,0:T(8,128)(2,1)} %param.8), kind=kLoop, calls=%fused_computation.88 | loop fusion | bytes 786432 | tf_op jit(solution)/shard_map/slice | solution.py:14
  17.7 4.5 %collective-permute-start.1 = (bf16[256,3,128]{2,1,0:T(4,128)(2,1)S(1)}, bf16[256,3,128]{2,1,0:T(4,128)(2,1)S(1)}, u32[]{:S(2)}, u32[]{:S(2)}) collective-permute-start(bf16[256,3,128]{2,1,0:T(4,128)(2,1)S(1)} %get-tuple-element.18), channel_id=1, source_target_pairs={{1,0},{2,1},{3,2},{4,3},{5,4},{6,5},{7,6},{8,7},{9,8},{10,9},{11,1... | collective-permute-start | bytes 589832 | tf_op jit(solution)/shard_map/ppermute | solution.py:19
  22.9 3.1 %collective-permute-done.1 = bf16[256,3,128]{2,1,0:T(4,128)(2,1)S(1)} collective-permute-done((bf16[256,3,128]{2,1,0:T(4,128)(2,1)S(1)}, bf16[256,3,128]{2,1,0:T(4,128)(2,1)S(1)}, u32[]{:S(2)}, u32[]{:S(2)}) %collective-permute-start.1) | collective-permute-done | bytes 196640 | tf_op jit(solution)/shard_map/ppermute | solution.py:19
  26.0 2.1 %maximum_convert_fusion = f32[256,22,128]{2,1,0:T(8,128)S(1)} fusion(bf16[256,3,128]{2,1,0:T(4,128)(2,1)S(1)} %collective-permute-done.1, bf16[256,16,128]{2,1,0:T(8,128)(2,1)} %param.8, bf16[256,3,128]{2,1,0:T(4,128)(2,1)S(1)} %collective-permute-done), kind=kLoop, calls=%fused_computation.30 | loop fusion | flops 4325376 | bytes 4325376 | tf_op jit(solution)/shard_map/convert_element_type | solution.py:82
  28.1 1.1 fusion.43
  29.2 1.1 fusion.44
  30.3 2.6 %fusion.4 = f32[256,20,128]{2,1,0:T(8,128)S(1)} fusion(f32[256,20,1]{2,1,0:T(8,128)S(1)} %get-tuple-element.14, f32[256,20,127]{2,1,0:T(8,128)S(1)} %get-tuple-element.16, f32[256,20,127]{2,1,0:T(8,128)S(1)} %get-tuple-element.15, f32[256,20,1]{2,1,0:T(8,128)S(1)} %get-tuple-element.13, f32[256,22,128]{2,1,0:T(8,128)S(1)} %maximum_convert_fusion, ...), kind=kLoop, calls=%fused_computation.6 | loop fusion | flops 7864320 | bytes 15749120 | tf_op jit(solution)/shard_map/sub | solution.py:33
  33.0 1.1 fusion.41
  34.1 1.1 fusion.42
  35.2 2.6 %fusion.9 = f32[256,18,128]{2,1,0:T(8,128)S(1)} fusion(f32[256,18,1]{2,1,0:T(8,128)S(1)} %get-tuple-element.10, f32[256,18,127]{2,1,0:T(8,128)S(1)} %get-tuple-element.12, f32[256,18,127]{2,1,0:T(8,128)S(1)} %get-tuple-element.11, f32[256,18,1]{2,1,0:T(8,128)S(1)} %get-tuple-element.9, f32[256,20,128]{2,1,0:T(8,128)S(1)} %fusion.4, ...), kind=kLoop, calls=%fused_computation.12 | loop fusion | flops 7077888 | bytes 14174208 | tf_op jit(solution)/shard_map/sub | solution.py:33
  38.6 0.8 fusion.40
  39.4 1.9 %fusion.19 = bf16[256,16,128]{2,1,0:T(8,128)(2,1)S(1)} fusion(f32[256,16,1]{2,1,0:T(8,128)S(1)} %get-tuple-element.6, f32[256,16,127]{2,1,0:T(8,128)S(1)} %get-tuple-element.8, f32[256,16,127]{2,1,0:T(8,128)S(1)} %get-tuple-element.7, f32[256,16,1]{2,1,0:T(8,128)S(1)} %get-tuple-element.5, f32[256,18,128]{2,1,0:T(8,128)S(1)} %fusion.9, ...), kind=kLoop, calls=%fused_computation.23 | loop fusion | flops 6815744 | bytes 11550720 | tf_op jit(solution)/shard_map/convert_element_type | solution.py:91
  41.5 1.2 %copy.12 = bf16[256,2,1024]{2,0,1:T(8,128)(2,1)} copy(bf16[256,2,1024]{2,1,0:T(2,128)(2,1)S(1)} %reshape.136) | data formatting | bytes 2097152 | tf_op jit(solution)/shard_map/reshape | solution.py:95
  42.8 3.8 %all-to-all-start = ((bf16[256,2,1024]{2,0,1:T(8,128)(2,1)}), bf16[256,2,1024]{2,0,1:T(8,128)(2,1)S(1)}, u32[]{:S(2)}, u32[]{:S(2)}) async-start(bf16[256,2,1024]{2,0,1:T(8,128)(2,1)} %copy.12), calls=%async_computation | async-start | bytes 2097152 | tf_op jit(solution)/shard_map/all_to_all | solution.py:98
  46.6 10.7 %all-to-all-done = bf16[256,2,1024]{2,0,1:T(8,128)(2,1)S(1)} async-done(((bf16[256,2,1024]{2,0,1:T(8,128)(2,1)}), bf16[256,2,1024]{2,0,1:T(8,128)(2,1)S(1)}, u32[]{:S(2)}, u32[]{:S(2)}) %all-to-all-start) | async-done | bytes 1048608 | tf_op jit(solution)/shard_map/all_to_all | solution.py:98
  57.8 1.2 %gather_fusion = bf16[256,512]{1,0:T(8,128)(2,1)S(1)} fusion(bf16[512,1024]{0,1:T(8,128)(2,1)S(1)} %copy.13, s32[1024]{0:T(1024)S(1)} %pad_clamp_fusion), kind=kCustom, calls=%fused_computation | custom fusion | bytes 525312 | tf_op jit(solution)/shard_map/jit(_take)/gather | solution.py:101
  59.1 4.4 %collective-permute-start.5 = (bf16[1,512,256]{1,2,0:T(8,128)(2,1)S(1)}, bf16[1,512,256]{1,2,0:T(8,128)(2,1)S(1)}, u32[]{:S(2)}, u32[]{:S(2)}) collective-permute-start(bf16[1,512,256]{1,2,0:T(8,128)(2,1)S(1)} %bitcast_select_fusion), channel_id=1, source_target_pairs={{1,0},{2,1},{3,2},{4,3},{5,4},{6,5},{7,6},{8,7},{9,8},{10,9},{11,1... | collective-permute-start | bytes 786440 | tf_op jit(solution)/shard_map/ppermute | solution.py:19
  63.9 3.9 %collective-permute-done.4 = bf16[1,512,256]{1,2,0:T(8,128)(2,1)S(1)} collective-permute-done((bf16[1,512,256]{1,2,0:T(8,128)(2,1)S(1)}, bf16[1,512,256]{1,2,0:T(8,128)(2,1)S(1)}, u32[]{:S(2)}, u32[]{:S(2)}) %collective-permute-start.4) | collective-permute-done | bytes 262176 | tf_op jit(solution)/shard_map/ppermute | solution.py:17
  67.9 4.1 %multiply_reduce_fusion = (f32[]{:T(128)}, f32[512,512]{1,0:T(8,128)S(1)}) fusion(f32[768]{0:T(1024)S(1)} %get-tuple-element.26, bf16[512,256]{0,1:T(8,128)(2,1)S(1)} %bitcast.79, bf16[512,256]{0,1:T(8,128)(2,1)S(1)} %bitcast.76, bf16[512,256]{0,1:T(8,128)(2,1)S(1)} %bitcast_select_fusion.1, f32[768]{0:T(1024)S(1)} %pad_maximum_fusion.4), kind=kOutput, calls=%fused_computation.39 | convolution fusion | flops 2423128064 | bytes 1841156 | tf_op jit(solution)/shard_map/dot_general | solution.py:48
  72.7 1.1 select_subtract_fusion.1
  73.8 1.9 %fusion.34 = f32[512,512]{1,0:T(8,128)S(1)} fusion(f32[512,512]{1,0:T(8,128)S(1)} %select_subtract_fusion.1, f32[512,512]{1,0:T(8,128)S(1)} %get-tuple-element.32, f32[]{:T(128)S(6)} %sqrt.6), kind=kOutput, calls=%fused_computation.51 | convolution fusion | flops 1610874880 | bytes 3145732 | tf_op jit(solution)/shard_map/dot_general | solution.py:59
  75.7 1.0 fusion.26
  76.7 1.1 fusion.23
  77.8 1.9 %select_subtract_fusion = f32[512,512]{1,0:T(8,128)S(1)} fusion(f32[512,512]{1,0:T(8,128)S(1)} %fusion.26, f32[512,512]{1,0:T(8,128)S(1)} %fusion.34), kind=kOutput, calls=%fused_computation.31 | convolution fusion | flops 1611661312 | bytes 3145728 | tf_op jit(solution)/shard_map/dot_general | solution.py:56
  79.7 2.1 %fusion.46 = f32[512,512]{1,0:T(8,128)S(1)} fusion(f32[512,512]{1,0:T(8,128)S(1)} %select_subtract_fusion, f32[512,512]{1,0:T(8,128)S(1)} %fusion.26), kind=kOutput, calls=%fused_computation.89 | convolution fusion | flops 1610612736 | bytes 3145728 | tf_op jit(solution)/shard_map/dot_general | solution.py:60
  81.8 1.0 convolution_bitcast_fusion
  82.8 1.0 fusion.47
  83.9 0.8 add_bitcast_fusion
  85.2 28.0 %all_to_all.33 = f32[512,8,128]{2,1,0:T(8,128)S(1)} all-to-all(f32[512,8,128]{2,1,0:T(8,128)S(1)} %bitcast.73), channel_id=1, replica_groups=mesh['mem'=2,'reg'=16] {'mem'}, dimensions={0} | all-to-all | bytes 4194304 | tf_op jit(solution)/shard_map/all_to_all | solution.py:121
  113.2 1.5 %copy.17 = f32[2,256,8,128]{3,2,0,1:T(8,128)} copy(f32[2,256,8,128]{3,2,1,0:T(8,128)S(1)} %bitcast.74) | data formatting | bytes 4194304 | tf_op jit(solution)/shard_map/all_to_all | solution.py:121
  (39 shorter events, 9.6 us)
Async XLA Ops:
  2.1 44.5 %collective-permute-start.6 = (bf16[1,2,256]{2,1,0:T(2,128)(2,1)S(1)}, bf16[1,2,256]{2,1,0:T(2,128)(2,1)S(1)}, u32[]{:S(2)}, u32[]{:S(2)}) collective-permute-start(bf16[1,2,256]{2,1,0:T(2,128)(2,1)S(1)} %maximum_bitcast_fusion), channel_id=1, source_target_pairs={{0,1},{1,2},{2,3},{3,4},{4,5},{5,6},{6,7},{7,8},{8,9},{9,10},{10,1... | collective-permute-start | bytes 3080 | tf_op jit(solution)/shard_map/ppermute | solution.py:17
  2.5 44.1 %collective-permute-start.7 = (bf16[1,2,256]{2,1,0:T(2,128)(2,1)S(1)}, bf16[1,2,256]{2,1,0:T(2,128)(2,1)S(1)}, u32[]{:S(2)}, u32[]{:S(2)}) collective-permute-start(bf16[1,2,256]{2,1,0:T(2,128)(2,1)S(1)} %maximum_bitcast_fusion), channel_id=1, source_target_pairs={{1,0},{2,1},{3,2},{4,3},{5,4},{6,5},{7,6},{8,7},{9,8},{10,9},{11,1... | collective-permute-start | bytes 3080 | tf_op jit(solution)/shard_map/ppermute | solution.py:19
  8.3 9.4 %collective-permute-start.2 = (f32[2,3,128]{2,1,0:T(4,128)S(1)}, f32[2,3,128]{2,1,0:T(4,128)S(1)}, u32[]{:S(2)}, u32[]{:S(2)}) collective-permute-start(f32[2,3,128]{2,1,0:T(4,128)S(1)} %get-tuple-element.23), channel_id=1, source_target_pairs={{0,1},{1,2},{2,3},{3,4},{4,5},{5,6},{6,7},{7,8},{8,9},{9,10},{10,1... | collective-permute-start | bytes 9224 | tf_op jit(solution)/shard_map/ppermute | solution.py:17
  8.3 13.8 %collective-permute-start.3 = (f32[2,3,128]{2,1,0:T(4,128)S(1)}, f32[2,3,128]{2,1,0:T(4,128)S(1)}, u32[]{:S(2)}, u32[]{:S(2)}) collective-permute-start(f32[2,3,128]{2,1,0:T(4,128)S(1)} %get-tuple-element.24), channel_id=1, source_target_pairs={{1,0},{2,1},{3,2},{4,3},{5,4},{6,5},{7,6},{8,7},{9,8},{10,9},{11,1... | collective-permute-start | bytes 9224 | tf_op jit(solution)/shard_map/ppermute | solution.py:19
  14.1 8.7 %collective-permute-start = (bf16[256,3,128]{2,1,0:T(4,128)(2,1)S(1)}, bf16[256,3,128]{2,1,0:T(4,128)(2,1)S(1)}, u32[]{:S(2)}, u32[]{:S(2)}) collective-permute-start(bf16[256,3,128]{2,1,0:T(4,128)(2,1)S(1)} %get-tuple-element.17), channel_id=1, source_target_pairs={{0,1},{1,2},{2,3},{3,4},{4,5},{5,6},{6,7},{7,8},{8,9},{9,10},{10,1... | collective-permute-start | bytes 589832 | tf_op jit(solution)/shard_map/ppermute | solution.py:17
  17.7 8.4 %collective-permute-start.1 = (bf16[256,3,128]{2,1,0:T(4,128)(2,1)S(1)}, bf16[256,3,128]{2,1,0:T(4,128)(2,1)S(1)}, u32[]{:S(2)}, u32[]{:S(2)}) collective-permute-start(bf16[256,3,128]{2,1,0:T(4,128)(2,1)S(1)} %get-tuple-element.18), channel_id=1, source_target_pairs={{1,0},{2,1},{3,2},{4,3},{5,4},{6,5},{7,6},{8,7},{9,8},{10,9},{11,1... | collective-permute-start | bytes 589832 | tf_op jit(solution)/shard_map/ppermute | solution.py:19
  38.6 0.8 copy-start
  42.8 14.5 %all-to-all-start = ((bf16[256,2,1024]{2,0,1:T(8,128)(2,1)}), bf16[256,2,1024]{2,0,1:T(8,128)(2,1)S(1)}, u32[]{:S(2)}, u32[]{:S(2)}) async-start(bf16[256,2,1024]{2,0,1:T(8,128)(2,1)} %copy.12), calls=%async_computation | async-start | bytes 2097152 | tf_op jit(solution)/shard_map/all_to_all | solution.py:98
  59.1 8.7 %collective-permute-start.4 = (bf16[1,512,256]{1,2,0:T(8,128)(2,1)S(1)}, bf16[1,512,256]{1,2,0:T(8,128)(2,1)S(1)}, u32[]{:S(2)}, u32[]{:S(2)}) collective-permute-start(bf16[1,512,256]{1,2,0:T(8,128)(2,1)S(1)} %bitcast_select_fusion), channel_id=1, source_target_pairs={{0,1},{1,2},{2,3},{3,4},{4,5},{5,6},{6,7},{7,8},{8,9},{9,10},{10,1... | collective-permute-start | bytes 786440 | tf_op jit(solution)/shard_map/ppermute | solution.py:17
  59.1 8.6 %collective-permute-start.5 = (bf16[1,512,256]{1,2,0:T(8,128)(2,1)S(1)}, bf16[1,512,256]{1,2,0:T(8,128)(2,1)S(1)}, u32[]{:S(2)}, u32[]{:S(2)}) collective-permute-start(bf16[1,512,256]{1,2,0:T(8,128)(2,1)S(1)} %bitcast_select_fusion), channel_id=1, source_target_pairs={{1,0},{2,1},{3,2},{4,3},{5,4},{6,5},{7,6},{8,7},{9,8},{10,9},{11,1... | collective-permute-start | bytes 786440 | tf_op jit(solution)/shard_map/ppermute | solution.py:19
where the time goes:
time: 115 us
  blocking collectives  28 us (24%)
  starting transfers between devices  22.7 us (20%)
  waiting for transfers between devices  17.7 us (15%)
  other arithmetic  16.1 us (14%)
  matrix products  15.9 us (14%)
  local copies, waits for them, and re-layouts  12.5 us (11%)
  between operations  1.73 us (2%)
    all_to_all x1, blocking collectives, on_device(): lax.all_to_all(shaped_back, 'mem', split_axis=0, concat_axis=1, tiled=True)  28 us
    ppermute x4, starting transfers between devices, with_halo(): lax.ppermute(head, axis, [((i + 1) % count, i) for i in range(count)])  18.4 us
    all_to_all x1, waiting for transfers between devices, on_device(): lax.all_to_all(refolded_values, 'mem', split_axis=1, concat_axis=0, tiled...  10.7 us
    slice x6, local copies, waits for them, and re-layouts, advance(): west_cell = jnp.roll(centre, 1, 2)  5.94 us
    sub x2, other arithmetic, advance(): centre + diffusion * (north_row + south_row + east_cell + west_cell - 4.0...  5.25 us
    dot_general x1, matrix products, analyse(): jnp.dot(weighted, obs_perturb.T, precision=lax.Precision.HIGHEST)  4.06 us
    ppermute x4, waiting for transfers between devices, with_halo(): lax.ppermute(tail, axis, [(i, (i + 1) % count) for i in range(count)])  3.87 us
    all_to_all x1, starting transfers between devices, on_device(): lax.all_to_all(refolded_values, 'mem', split_axis=1, concat_axis=0, tiled...  3.76 us
  transfers between devices with their start and end apart: 9, of which 3 were waited for; matrix products, arithmetic and copies ran while one was open for 20% of the time, Pallas kernels for 0%

commit v1 on v0

v1 whole, which is shorter than its diff:
```python
import functools

import jax
import jax.numpy as jnp
from jax import lax
from jax.experimental import pallas as pl
from jax.experimental.pallas import tpu as pltpu
from jax.sharding import PartitionSpec as P

STEPS = 3
MESH = pl.DeviceIdType.MESH
F32 = jnp.float32
BF16 = jnp.bfloat16
MEMBER_BLOCK = 64


def kernel(
    groups, regions,
    mem_ref, dif_ref, adv_ref, val_ref, rinv_ref, cell_ref, cnt_ref, loc_ref,
    out_ref,
    padded, first, second, fc, states, coef, coef_in, cells_out, cells_in,
    info_out, info_in, hsend, hall, wt, xb, xbar, ret_out, ret_in,
    local_sem, send_sem, recv_sem,
):
    lines, local, width = mem_ref.shape
    patch = lines // groups
    slots = hall.shape[2]
    members = groups * local
    halo = STEPS
    m = lax.axis_index("mem")
    r = lax.axis_index("reg")
    up = lax.rem(r + regions - 1, regions)
    down = lax.rem(r + 1, regions)

    barrier = pltpu.get_barrier_semaphore()
    for side in (up, down):
        pl.semaphore_signal(barrier, inc=1, device_id=(m, side), device_id_type=MESH)
    for j in range(1, groups):
        pl.semaphore_signal(barrier, inc=1, device_id=(lax.rem(m + j, groups), r), device_id_type=MESH)
    own_load = pltpu.make_async_copy(mem_ref, padded.at[pl.ds(halo, lines)], local_sem.at[0])
    own_load.start()
    cells_out[...] = jnp.broadcast_to(cell_ref[0], cells_out.shape)
    slot = lax.broadcasted_iota(jnp.int32, (1, slots), 1)
    own_prec = jnp.where(slot < cnt_ref[...], rinv_ref[0], 0.0)
    reach = (loc_ref[0].astype(F32) + 1.0) * 0.25
    far_prec = (own_prec * jnp.exp(-(reach * reach))).astype(BF16).astype(F32)
    own_val = val_ref[0].astype(F32)
    info_row = lax.broadcasted_iota(jnp.int32, info_out.shape, 0)
    info_out[...] = jnp.where(info_row == 0, own_val, far_prec)
    pl.semaphore_wait(barrier, groups + 1)

    copies = []

    def send(src, dst, target):
        at = len(copies)
        copy = pltpu.make_async_remote_copy(
            src_ref=src, dst_ref=dst, send_sem=send_sem.at[at], recv_sem=recv_sem.at[at],
            device_id=target, device_id_type=MESH,
        )
        copy.start()
        copies.append(copy)
        return copy

    above, below = (m, up), (m, down)
    halo_top = send(mem_ref.at[pl.ds(lines - halo, halo)], padded.at[pl.ds(0, halo)], below)
    halo_bottom = send(mem_ref.at[pl.ds(0, halo)], padded.at[pl.ds(lines + halo, halo)], above)
    coef_top = [
        send(ref.at[pl.ds(lines - 8, 8)], coef_in.at[0, i], below)
        for i, ref in enumerate((dif_ref, adv_ref))
    ]
    coef_bottom = [
        send(ref.at[pl.ds(0, 8)], coef_in.at[1, i], above)
        for i, ref in enumerate((dif_ref, adv_ref))
    ]
    cell_copies = [
        send(cells_out, cells_in.at[j - 1], (lax.rem(m + j, groups), r)) for j in range(1, groups)
    ]
    info_copies = [
        send(info_out, info_in.at[0], below),
        send(info_out, info_in.at[1], above),
    ]

    def put_coef(base, d, a):
        rows = pl.ds(base, d.shape[0])
        coef[0, rows] = 1.0 - 4.0 * d
        coef[1, rows] = d + 0.5 * a
        coef[2, rows] = d - 0.5 * a
        coef[3, rows] = d

    put_coef(8, dif_ref[...], adv_ref[...])

    def step(src, dst, shift, low, high):
        def body(p, _):
            k = [coef[i, pl.ds(p + 8 - halo, 1), :] for i in range(4)]
            for at in range(0, local, MEMBER_BLOCK):
                block = pl.ds(at, MEMBER_BLOCK)
                c = src[p, block, :].astype(F32)
                n = src[p - 1, block, :].astype(F32)
                s = src[p + 1, block, :].astype(F32)
                sides = pltpu.roll(c, width - 1, 1) + pltpu.roll(c, 1, 1)
                value = k[0] * c + k[1] * n + k[2] * s + k[3] * sides
                dst[p - shift, block, :] = value.astype(dst.dtype)
            return 0

        lax.fori_loop(low, high, body, 0)

    own_load.wait()
    step(padded, first, 0, 4, lines + 2)
    step(first, second, 0, 5, lines + 1)
    step(second, fc, halo, 6, lines)

    def forward(early):
        made = []
        for j in range(1, groups):
            g = lax.rem(m + j, groups)
            inner = (g + groups - 1) // groups
            if early:
                at, count = halo * (1 - inner), patch - halo
            else:
                at, count = (patch - halo) * inner, halo
            made.append(send(
                fc.at[pl.ds(g * patch + at, count)],
                states.at[pl.ds(at, count), pl.ds(m * local, local)],
                (g, r),
            ))
        return made

    forwards = forward(True)

    halo_top.wait_recv()
    for copy in coef_top:
        copy.wait_recv()
    put_coef(0, coef_in[0, 0], coef_in[0, 1])
    step(padded, first, 0, 1, 4)
    step(first, second, 0, 2, 5)
    step(second, fc, halo, 3, 6)
    halo_bottom.wait_recv()
    for copy in coef_bottom:
        copy.wait_recv()
    put_coef(lines + 8, coef_in[1, 0], coef_in[1, 1])
    step(padded, first, 0, lines + 2, lines + 5)
    step(first, second, 0, lines + 1, lines + 4)
    step(second, fc, halo, lines, lines + 3)

    cell_index = lax.broadcasted_iota(jnp.int32, (patch * width, slots), 0)

    def observe(g, cells):
        flat = jnp.concatenate([fc[g * patch + l] for l in range(patch)], axis=1)
        pick = jnp.where(cell_index == cells, 1.0, 0.0).astype(BF16)
        return jnp.dot(flat, pick, preferred_element_type=F32).astype(BF16)

    hx = []
    for j in range(1, groups):
        g = lax.rem(m + groups - j, groups)
        cell_copies[j - 1].wait_recv()
        hsend[j - 1] = observe(g, cells_in[j - 1, 0:1, :])
        hx.append(send(hsend.at[j - 1], hall.at[0, pl.ds(m * local, local)], (g, r)))
    forwards += forward(False)
    own_rows = pl.ds(pl.multiple_of(m * local, local), local)
    hall[0, own_rows, :] = observe(m, cell_ref[0])

    def relay(block):
        rows = pl.ds(block * local, local)
        return [
            send(hall.at[0, rows], hall.at[1, rows], below),
            send(hall.at[0, rows], hall.at[2, rows], above),
        ]

    relays = relay(m)
    for l in range(patch):
        states[l, own_rows, :] = fc[m * patch + l]
    for j in range(1, groups):
        hx[j - 1].wait_recv()
        relays += relay(lax.rem(m + j, groups))

    row_id = lax.broadcasted_iota(jnp.int32, (members, members), 0)
    col_id = lax.broadcasted_iota(jnp.int32, (members, members), 1)
    eye = jnp.where(row_id == col_id, 1.0, 0.0)

    def gram(h, value, prec):
        h = h.astype(F32)
        hbar = jnp.sum(h, axis=0, keepdims=True) * (1.0 / members)
        y = h - hbar
        weighted = y * prec
        part = lax.dot_general(
            weighted.astype(BF16), y.astype(BF16), (((1,), (1,)), ((), ())),
            preferred_element_type=F32,
        )
        return part, jnp.sum(weighted * (value - hbar), axis=1, keepdims=True)

    system, force = gram(hall[0], own_val, own_prec)
    system = system + (members - 1.0) * eye
    for copy in info_copies + relays:
        copy.wait_recv()
    for side in range(2):
        part, more = gram(hall[1 + side], info_in[side, 0:1, :], info_in[side, 1:2, :])
        system, force = system + part, force + more
    total = jnp.sum(jnp.sum(system * system, axis=0, keepdims=True), axis=1, keepdims=True)
    inv_scale = lax.rsqrt(total)
    y1 = system * inv_scale
    y1b = y1.astype(BF16)
    y2 = jnp.dot(y1b, y1b, preferred_element_type=F32)
    tail = (0.0625 * y2 - 0.5625 * y1).astype(BF16)
    z = 2.25 * eye - 2.4375 * y1 + 1.6875 * y2 + jnp.dot(
        y2.astype(BF16), tail, preferred_element_type=F32
    )
    half = jnp.sum(z * force, axis=0, keepdims=True)
    mean_col = jnp.sum(z * half, axis=1, keepdims=True) * inv_scale
    mean_row = jnp.sum(eye * mean_col, axis=0, keepdims=True)
    wt[...] = (jnp.sqrt((members - 1.0) * inv_scale) * z + mean_row).astype(BF16)

    for copy in forwards:
        copy.wait_recv()
    for l in range(patch):
        lane = pl.ds(l * width, width)
        x = states[l].astype(F32)
        mean = jnp.sum(x, axis=0, keepdims=True) * (1.0 / members)
        xbar[0:1, lane] = mean
        xb[:, lane] = (x - mean).astype(BF16)

    def result(g, l, count):
        lane = pl.ds(l * width, count * width)
        rows = pl.ds(pl.multiple_of(g * local, local), local)
        return xbar[0:1, lane] + jnp.dot(wt[rows, :], xb[:, lane], preferred_element_type=F32)

    pair = 2
    returns = []
    for l in range(0, patch, pair):
        for j in range(1, groups):
            g = lax.rem(m + j, groups)
            value = result(g, l, pair).astype(BF16)
            for i in range(pair):
                ret_out[j - 1, l + i] = value[:, i * width:(i + 1) * width]
            rows = pl.ds(l, pair)
            returns.append((j, l, send(ret_out.at[j - 1, rows], ret_in.at[j - 1, rows], (g, r))))
    for l in range(0, patch, pair):
        value = result(m, l, pair)
        for i in range(pair):
            out_ref[m * patch + l + i] = value[:, i * width:(i + 1) * width]
    for j, l, copy in returns:
        copy.wait_recv()
        g = lax.rem(m + groups - j, groups)
        for i in range(pair):
            out_ref[g * patch + l + i] = ret_in[j - 1, l + i].astype(F32)
    for copy in copies:
        copy.wait_send()


def on_device(groups, regions, members, diffusivity, advection, obs_value, obs_rinv, obs_cell, obs_count, loc_index):
    local, lines, width = members.shape
    slots = obs_cell.shape[-1]
    patch = lines // groups
    total = groups * local
    partners = groups - 1
    pairs = patch // 2
    count = 8 + partners + 2 * partners + partners + 2 * groups + partners * pairs
    vmem = pl.BlockSpec(memory_space=pltpu.VMEM)
    flops = 2 * total * total * (3 * slots + 2 * total + patch * width)
    result = pl.pallas_call(
        functools.partial(kernel, groups, regions),
        out_shape=jax.ShapeDtypeStruct((lines, local, width), F32),
        in_specs=[pl.BlockSpec(memory_space=pl.ANY)] + [vmem] * 7,
        out_specs=vmem,
        scratch_shapes=[
            pltpu.VMEM((lines + 2 * STEPS, local, width), BF16),
            pltpu.VMEM((lines + 2 * STEPS, local, width), F32),
            pltpu.VMEM((lines + 2 * STEPS, local, width), F32),
            pltpu.VMEM((lines, local, width), BF16),
            pltpu.VMEM((patch, total, width), BF16),
            pltpu.VMEM((4, lines + 16, width), F32),
            pltpu.VMEM((2, 2, 8, width), F32),
            pltpu.VMEM((8, slots), jnp.int32),
            pltpu.VMEM((partners, 8, slots), jnp.int32),
            pltpu.VMEM((8, slots), F32),
            pltpu.VMEM((2, 8, slots), F32),
            pltpu.VMEM((partners, local, slots), BF16),
            pltpu.VMEM((3, total, slots), BF16),
            pltpu.VMEM((total, total), BF16),
            pltpu.VMEM((total, patch * width), BF16),
            pltpu.VMEM((8, patch * width), F32),
            pltpu.VMEM((partners, patch, local, width), BF16),
            pltpu.VMEM((partners, patch, local, width), BF16),
            pltpu.SemaphoreType.DMA((1,)),
            pltpu.SemaphoreType.DMA((count,)),
            pltpu.SemaphoreType.DMA((count,)),
        ],
        compiler_params=pltpu.CompilerParams(
            collective_id=0, has_side_effects=True, vmem_limit_bytes=48 * 1024 * 1024
        ),
        cost_estimate=pl.CostEstimate(flops=flops, bytes_accessed=6 * lines * local * width, transcendentals=0),
    )(
        jnp.transpose(members, (1, 0, 2)), diffusivity, advection, obs_value, obs_rinv,
        obs_cell, obs_count, loc_index,
    )
    return jnp.transpose(result, (1, 0, 2))


def solution(mesh):
    return jax.shard_map(
        functools.partial(on_device, mesh.shape["mem"], mesh.shape["reg"]),
        mesh=mesh,
        in_specs=(
            P("mem", "reg", None),
            P("reg", None),
            P("reg", None),
            P("reg", "mem", None),
            P("reg", "mem", None),
            P("reg", "mem", None),
            P("reg", "mem"),
            P("reg", "mem", None),
        ),
        out_specs=P("mem", "reg", None),
        check_vma=False,
    )
```

time: 115 us -> 46.2 us (0.40)
  Pallas kernels: 0 us -> 41.2 us
  blocking collectives: 28 us -> 0 us
  starting transfers between devices: 22.7 us -> 0 us
  waiting for transfers between devices: 17.7 us -> 0 us
  other arithmetic: 16.1 us -> 0 us
  matrix products: 15.9 us -> 0 us
  local copies, waits for them, and re-layouts: 12.5 us -> 4.06 us
    pallas_call x0 -> x1, Pallas kernels: none -> 41.2 us  [on_device(): pl.pallas_call(functools.partial(kernel, groups, regions), out_shape=jax....]
    all_to_all x1 -> x0, blocking collectives: 28 us -> none  [on_device(): lax.all_to_all(shaped_back, 'mem', split_axis=0, concat_axis=1, tiled=True)]
    ppermute x8 -> x0, starting transfers between devices: 19 us -> none  [the longest x4 18.4 us: with_halo(): lax.ppermute(head, axis, [((i + 1) % count, i) for i in range(count)])]
    dot_general x10 -> x0, matrix products: 15.9 us -> none  [the longest x1 4.06 us: analyse(): jnp.dot(weighted, obs_perturb.T, precision=lax.Precision.HIGHEST)]
    all_to_all x1 -> x0, waiting for transfers between devices: 10.7 us -> none  [on_device(): lax.all_to_all(refolded_values, 'mem', split_axis=1, concat_axis=0, tiled...]
    slice x7 -> x0, local copies, waits for them, and re-layouts: 7.34 us -> none  [the longest x6 5.94 us: advance(): west_cell = jnp.roll(centre, 1, 2)]
    ppermute x8 -> x0, waiting for transfers between devices: 7.01 us -> none  [the longest x4 3.87 us: with_halo(): lax.ppermute(tail, axis, [(i, (i + 1) % count) for i in range(count)])]
    sub x3 -> x0, other arithmetic: 5.26 us -> none  [the longest x2 5.25 us: advance(): centre + diffusion * (north_row + south_row + east_cell + west_cell - 4.0...]
  transfers between devices with their start and end apart: 9 -> 0, of which waited for: 3 -> 0; matrix products, arithmetic and copies ran while one was open for 20% -> 0% of each run, Pallas kernels for 0% -> 0%
where the time goes in v1:
time: 46.2 us; the launch traced here: 46 us
  Pallas kernels  41.2 us (89%)
  local copies, waits for them, and re-layouts  4.06 us (9%)
  between operations  0.8 us (2%)
    pallas_call x1, Pallas kernels, on_device(): pl.pallas_call(functools.partial(kernel, groups, regions), out_shape=jax....  41.2 us
    transpose x1, local copies, waits for them, and re-layouts, on_device(): return jnp.transpose(result, (1, 0, 2))  2.54 us
    unnamed x13, local copies, waits for them, and re-layouts  1.52 us

profile of v1, /device:TPU:0, one launch (start us, length us, event | category | flops | bytes accessed | tf_op | source)
XLA Modules:
  0.0 46.0 jit_solution(8429799165263288014)
XLA Ops:
  0.0 0.0 copy-start.5
  0.0 0.0 copy-start.4
  0.0 0.0 copy-start.3
  0.0 0.0 copy-start.2
  0.0 0.0 copy-start.1
  0.0 0.0 copy-start
  0.7 1.5 %copy.12 = bf16[256,16,128]{2,0,1:T(8,128)(2,1)S(1)} copy(bf16[256,16,128]{2,1,0:T(8,128)(2,1)} %param.8) | data formatting | bytes 2097152 | tf_op args[0]
  2.2 0.0 copy-done.5
  2.3 0.0 copy-done.4
  2.3 0.0 copy-done.3
  2.3 0.0 copy-done.2
  2.3 0.0 copy-done.1
  2.3 0.0 copy-done
  2.3 41.2 %shard_map.82 = f32[16,256,128]{2,1,0:T(8,128)S(1)} custom-call(bf16[16,256,128]{2,1,0:T(8,128)(2,1)S(1)} %bitcast.5, f32[16,128]{1,0:T(8,128)S(1)} %copy-done, f32[16,128]{1,0:T(8,128)S(1)} %copy-done.1, bf16[1,1,256]{2,1,0:T(2,128)(2,1)S(1)} %copy-done.2, f32[1,1,256]{2,1,0:T(1,128)S(1)} %copy-done.3, s32[1,1,256]{2,1,0:T(1,128)S(1)} %copy-done.4, ...), custom_call_target="tpu_custom_call" | custom-call | flops 1476395008 | bytes 3145728 | tf_op jit(solution)/shard_map/pallas_call | solution.py:259
  43.5 2.5 %copy.10 = f32[256,16,128]{2,1,0:T(8,128)} copy(f32[256,16,128]{2,0,1:T(8,128)S(1)} %bitcast.4) | data formatting | bytes 4194304 | tf_op jit(solution)/shard_map/transpose | solution.py:295
Async XLA Ops:
  0.0 2.2 %copy-start.5 = (s32[1,1,256]{2,1,0:T(1,128)S(1)}, s32[1,1,256]{2,1,0:T(1,128)}, u32[]{:S(2)}) copy-start(s32[1,1,256]{2,1,0:T(1,128)} %loc_ref.1) | copy-start | bytes 3076
  0.0 2.3 %copy-start.4 = (s32[1,1,256]{2,1,0:T(1,128)S(1)}, s32[1,1,256]{2,1,0:T(1,128)}, u32[]{:S(2)}) copy-start(s32[1,1,256]{2,1,0:T(1,128)} %cell_ref.1) | copy-start | bytes 3076
  0.0 2.3 %copy-start.3 = (f32[1,1,256]{2,1,0:T(1,128)S(1)}, f32[1,1,256]{2,1,0:T(1,128)}, u32[]{:S(2)}) copy-start(f32[1,1,256]{2,1,0:T(1,128)} %rinv_ref.1) | copy-start | bytes 3076
  0.0 2.3 %copy-start.2 = (bf16[1,1,256]{2,1,0:T(2,128)(2,1)S(1)}, bf16[1,1,256]{2,1,0:T(2,128)(2,1)}, u32[]{:S(2)}) copy-start(bf16[1,1,256]{2,1,0:T(2,128)(2,1)} %val_ref.1) | copy-start | bytes 1540
  0.0 2.3 %copy-start.1 = (f32[16,128]{1,0:T(8,128)S(1)}, f32[16,128]{1,0:T(8,128)}, u32[]{:S(2)}) copy-start(f32[16,128]{1,0:T(8,128)} %adv_ref.1) | copy-start | bytes 24580
  0.0 2.3 %copy-start = (f32[16,128]{1,0:T(8,128)S(1)}, f32[16,128]{1,0:T(8,128)}, u32[]{:S(2)}) copy-start(f32[16,128]{1,0:T(8,128)} %dif_ref.1) | copy-start | bytes 24580

commit v2 on v1

--- a/solution.py
+++ b/solution.py
@@ -105,42 +105,50 @@
         lax.fori_loop(low, high, body, 0)
 
     own_load.wait()
-    step(padded, first, 0, 4, lines + 2)
-    step(first, second, 0, 5, lines + 1)
-    step(second, fc, halo, 6, lines)
-
-    def forward(early):
-        made = []
-        for j in range(1, groups):
-            g = lax.rem(m + j, groups)
-            inner = (g + groups - 1) // groups
-            if early:
-                at, count = halo * (1 - inner), patch - halo
-            else:
-                at, count = (patch - halo) * inner, halo
-            made.append(send(
-                fc.at[pl.ds(g * patch + at, count)],
-                states.at[pl.ds(at, count), pl.ds(m * local, local)],
-                (g, r),
-            ))
-        return made
-
-    forwards = forward(True)
+
+    def early_at(g):
+        return halo * (1 - (g + groups - 1) // groups)
+
+    def late_at(g):
+        return (patch - halo) * ((g + groups - 1) // groups)
+
+    early = patch - halo
+
+    def interior(g):
+        low = g * patch + early_at(g) + halo
+        high = low + early
+        step(padded, first, 0, low - 2, high + 2)
+        step(first, second, 0, low - 1, high + 1)
+        step(second, fc, halo, low, high)
+
+    def edge(g):
+        inner = (g + groups - 1) // groups
+        end = g * patch + patch
+        for s, (src, dst, shift) in enumerate(((padded, first, 0), (first, second, 0), (second, fc, halo))):
+            low = (s - 2) * (1 - inner) + (end - 1 - s) * inner + halo
+            step(src, dst, shift, low, low + halo)
+
+    forwards = []
+
+    def forward(j, late, at, count):
+        g = lax.rem(m + j, groups)
+        at = at + (late_at(g) if late else early_at(g))
+        forwards.append((late, send(
+            fc.at[pl.ds(g * patch + at, count)],
+            states.at[pl.ds(at, count), pl.ds(m * local, local)],
+            (g, r),
+        )))
+
+    for j in range(1, groups):
+        interior(lax.rem(m + j, groups))
+        forward(j, False, 0, early - 2)
 
     halo_top.wait_recv()
-    for copy in coef_top:
+    halo_bottom.wait_recv()
+    for copy in coef_top + coef_bottom:
         copy.wait_recv()
     put_coef(0, coef_in[0, 0], coef_in[0, 1])
-    step(padded, first, 0, 1, 4)
-    step(first, second, 0, 2, 5)
-    step(second, fc, halo, 3, 6)
-    halo_bottom.wait_recv()
-    for copy in coef_bottom:
-        copy.wait_recv()
     put_coef(lines + 8, coef_in[1, 0], coef_in[1, 1])
-    step(padded, first, 0, lines + 2, lines + 5)
-    step(first, second, 0, lines + 1, lines + 4)
-    step(second, fc, halo, lines, lines + 3)
 
     cell_index = lax.broadcasted_iota(jnp.int32, (patch * width, slots), 0)
 
@@ -151,12 +159,15 @@
 
     hx = []
     for j in range(1, groups):
-        g = lax.rem(m + groups - j, groups)
-        cell_copies[j - 1].wait_recv()
-        hsend[j - 1] = observe(g, cells_in[j - 1, 0:1, :])
+        g = lax.rem(m + j, groups)
+        edge(g)
+        cell_copies[groups - j - 1].wait_recv()
+        hsend[j - 1] = observe(g, cells_in[groups - j - 1, 0:1, :])
         hx.append(send(hsend.at[j - 1], hall.at[0, pl.ds(m * local, local)], (g, r)))
-    forwards += forward(False)
+        forward(j, False, early - 2, 1)
     own_rows = pl.ds(pl.multiple_of(m * local, local), local)
+    interior(m)
+    edge(m)
     hall[0, own_rows, :] = observe(m, cell_ref[0])
 
     def relay(block):
@@ -171,7 +182,9 @@
         states[l, own_rows, :] = fc[m * patch + l]
     for j in range(1, groups):
         hx[j - 1].wait_recv()
-        relays += relay(lax.rem(m + j, groups))
+        relays += relay(lax.rem(m + groups - j, groups))
+        forward(j, False, early - 1, 1)
+        forward(j, True, 0, halo)
 
     row_id = lax.broadcasted_iota(jnp.int32, (members, members), 0)
     col_id = lax.broadcasted_iota(jnp.int32, (members, members), 1)
@@ -190,6 +203,18 @@
 
     system, force = gram(hall[0], own_val, own_prec)
     system = system + (members - 1.0) * eye
+
+    def perturb(low, count):
+        for i in range(count):
+            lane = pl.ds(pl.multiple_of((low + i) * width, width), width)
+            x = states[low + i].astype(F32)
+            mean = jnp.sum(x, axis=0, keepdims=True) * (1.0 / members)
+            xbar[0:1, lane] = mean
+            xb[:, lane] = (x - mean).astype(BF16)
+
+    for late, copy in forwards[:2 * (groups - 1)]:
+        copy.wait_recv()
+    perturb(early_at(m), early - 1)
     for copy in info_copies + relays:
         copy.wait_recv()
     for side in range(2):
@@ -209,38 +234,46 @@
     mean_row = jnp.sum(eye * mean_col, axis=0, keepdims=True)
     wt[...] = (jnp.sqrt((members - 1.0) * inv_scale) * z + mean_row).astype(BF16)
 
-    for copy in forwards:
-        copy.wait_recv()
-    for l in range(patch):
-        lane = pl.ds(l * width, width)
-        x = states[l].astype(F32)
-        mean = jnp.sum(x, axis=0, keepdims=True) * (1.0 / members)
-        xbar[0:1, lane] = mean
-        xb[:, lane] = (x - mean).astype(BF16)
-
     def result(g, l, count):
-        lane = pl.ds(l * width, count * width)
+        lane = pl.ds(pl.multiple_of(l * width, width), count * width)
         rows = pl.ds(pl.multiple_of(g * local, local), local)
         return xbar[0:1, lane] + jnp.dot(wt[rows, :], xb[:, lane], preferred_element_type=F32)
 
-    pair = 2
+    cuts = ((False, 0, early - 3), (False, early - 3, 2), (False, early - 1, 1), (True, 0, halo))
+
+    def row_of(g, cut):
+        return cut[1] + (late_at(g) if cut[0] else early_at(g))
+
     returns = []
-    for l in range(0, patch, pair):
+    for cut in cuts:
+        l, count = row_of(m, cut), cut[2]
+        if cut[0]:
+            for late, copy in forwards[2 * (groups - 1):]:
+                if late:
+                    copy.wait_recv()
+            perturb(late_at(m), halo)
+        elif cut[1] == early - 1:
+            for late, copy in forwards[2 * (groups - 1):]:
+                if not late:
+                    copy.wait_recv()
+            perturb(l, 1)
         for j in range(1, groups):
             g = lax.rem(m + j, groups)
-            value = result(g, l, pair).astype(BF16)
-            for i in range(pair):
+            value = result(g, l, count).astype(BF16)
+            for i in range(count):
                 ret_out[j - 1, l + i] = value[:, i * width:(i + 1) * width]
-            rows = pl.ds(l, pair)
-            returns.append((j, l, send(ret_out.at[j - 1, rows], ret_in.at[j - 1, rows], (g, r))))
-    for l in range(0, patch, pair):
-        value = result(m, l, pair)
-        for i in range(pair):
+            rows = pl.ds(l, count)
+            returns.append((j, cut, send(ret_out.at[j - 1, rows], ret_in.at[j - 1, rows], (g, r))))
+    for cut in cuts:
+        l, count = row_of(m, cut), cut[2]
+        value = result(m, l, count)
+        for i in range(count):
             out_ref[m * patch + l + i] = value[:, i * width:(i + 1) * width]
-    for j, l, copy in returns:
+    for j, cut, copy in returns:
         copy.wait_recv()
         g = lax.rem(m + groups - j, groups)
-        for i in range(pair):
+        l = row_of(g, cut)
+        for i in range(cut[2]):
             out_ref[g * patch + l + i] = ret_in[j - 1, l + i].astype(F32)
     for copy in copies:
         copy.wait_send()
@@ -252,8 +285,7 @@
     patch = lines // groups
     total = groups * local
     partners = groups - 1
-    pairs = patch // 2
-    count = 8 + partners + 2 * partners + partners + 2 * groups + partners * pairs
+    count = 8 + partners + 4 * partners + partners + 2 * groups + 4 * partners
     vmem = pl.BlockSpec(memory_space=pltpu.VMEM)
     flops = 2 * total * total * (3 * slots + 2 * total + patch * width)
     result = pl.pallas_call(

time: 46.2 us -> 44.6 us (0.965)
  Pallas kernels: 41.2 us -> 39.6 us
    pallas_call x1, Pallas kernels: 41.2 us -> 39.6 us  [on_device(): pl.pallas_call(functools.partial(kernel, groups, regions), out_shape=jax....]
where the time goes in v2:
time: 44.6 us; the launch traced here: 44.4 us
  Pallas kernels  39.6 us (89%)
  local copies, waits for them, and re-layouts  4.06 us (9%)
  between operations  0.8 us (2%)
    pallas_call x1, Pallas kernels, on_device(): pl.pallas_call(functools.partial(kernel, groups, regions), out_shape=jax....  39.6 us
    transpose x1, local copies, waits for them, and re-layouts, on_device(): return jnp.transpose(result, (1, 0, 2))  2.54 us
    unnamed x13, local copies, waits for them, and re-layouts  1.52 us

profile of v2, /device:TPU:0, one launch (start us, length us, event | category | flops | bytes accessed | tf_op | source)
XLA Modules:
  0.0 44.4 jit_solution(9701765936102592484)
XLA Ops:
  0.0 0.0 copy-start.5
  0.0 0.0 copy-start.4
  0.0 0.0 copy-start.3
  0.0 0.0 copy-start.2
  0.0 0.0 copy-start.1
  0.0 0.0 copy-start
  0.7 1.5 %copy.12 = bf16[256,16,128]{2,0,1:T(8,128)(2,1)S(1)} copy(bf16[256,16,128]{2,1,0:T(8,128)(2,1)} %param.8) | data formatting | bytes 2097152 | tf_op args[0]
  2.2 0.0 copy-done.5
  2.3 0.0 copy-done.4
  2.3 0.0 copy-done.3
  2.3 0.0 copy-done.2
  2.3 0.0 copy-done.1
  2.3 0.0 copy-done
  2.3 39.6 %shard_map.82 = f32[16,256,128]{2,1,0:T(8,128)S(1)} custom-call(bf16[16,256,128]{2,1,0:T(8,128)(2,1)S(1)} %bitcast.5, f32[16,128]{1,0:T(8,128)S(1)} %copy-done, f32[16,128]{1,0:T(8,128)S(1)} %copy-done.1, bf16[1,1,256]{2,1,0:T(2,128)(2,1)S(1)} %copy-done.2, f32[1,1,256]{2,1,0:T(1,128)S(1)} %copy-done.3, s32[1,1,256]{2,1,0:T(1,128)S(1)} %copy-done.4, ...), custom_call_target="tpu_custom_call" | custom-call | flops 1476395008 | bytes 3145728 | tf_op jit(solution)/shard_map/pallas_call | solution.py:291
  41.9 2.5 %copy.10 = f32[256,16,128]{2,1,0:T(8,128)} copy(f32[256,16,128]{2,0,1:T(8,128)S(1)} %bitcast.4) | data formatting | bytes 4194304 | tf_op jit(solution)/shard_map/transpose | solution.py:327
Async XLA Ops:
  0.0 2.2 %copy-start.5 = (s32[1,1,256]{2,1,0:T(1,128)S(1)}, s32[1,1,256]{2,1,0:T(1,128)}, u32[]{:S(2)}) copy-start(s32[1,1,256]{2,1,0:T(1,128)} %loc_ref.1) | copy-start | bytes 3076
  0.0 2.3 %copy-start.4 = (s32[1,1,256]{2,1,0:T(1,128)S(1)}, s32[1,1,256]{2,1,0:T(1,128)}, u32[]{:S(2)}) copy-start(s32[1,1,256]{2,1,0:T(1,128)} %cell_ref.1) | copy-start | bytes 3076
  0.0 2.3 %copy-start.3 = (f32[1,1,256]{2,1,0:T(1,128)S(1)}, f32[1,1,256]{2,1,0:T(1,128)}, u32[]{:S(2)}) copy-start(f32[1,1,256]{2,1,0:T(1,128)} %rinv_ref.1) | copy-start | bytes 3076
  0.0 2.3 %copy-start.2 = (bf16[1,1,256]{2,1,0:T(2,128)(2,1)S(1)}, bf16[1,1,256]{2,1,0:T(2,128)(2,1)}, u32[]{:S(2)}) copy-start(bf16[1,1,256]{2,1,0:T(2,128)(2,1)} %val_ref.1) | copy-start | bytes 1540
  0.0 2.3 %copy-start.1 = (f32[16,128]{1,0:T(8,128)S(1)}, f32[16,128]{1,0:T(8,128)}, u32[]{:S(2)}) copy-start(f32[16,128]{1,0:T(8,128)} %adv_ref.1) | copy-start | bytes 24580
  0.0 2.3 %copy-start = (f32[16,128]{1,0:T(8,128)S(1)}, f32[16,128]{1,0:T(8,128)}, u32[]{:S(2)}) copy-start(f32[16,128]{1,0:T(8,128)} %dif_ref.1) | copy-start | bytes 24580

commit v3 on v2

--- a/solution.py
+++ b/solution.py
@@ -47,6 +47,57 @@
     own_val = val_ref[0].astype(F32)
     info_row = lax.broadcasted_iota(jnp.int32, info_out.shape, 0)
     info_out[...] = jnp.where(info_row == 0, own_val, far_prec)
+    def put_coef(base, d, a):
+        rows = pl.ds(base, d.shape[0])
+        coef[0, rows] = 1.0 - 4.0 * d
+        coef[1, rows] = d + 0.5 * a
+        coef[2, rows] = d - 0.5 * a
+        coef[3, rows] = d
+
+    put_coef(8, dif_ref[...], adv_ref[...])
+
+    def step(src, dst, shift, low, high):
+        def body(p, _):
+            k = [coef[i, pl.ds(p + 8 - halo, 1), :] for i in range(4)]
+            for at in range(0, local, MEMBER_BLOCK):
+                block = pl.ds(at, MEMBER_BLOCK)
+                c = src[p, block, :].astype(F32)
+                n = src[p - 1, block, :].astype(F32)
+                s = src[p + 1, block, :].astype(F32)
+                sides = pltpu.roll(c, width - 1, 1) + pltpu.roll(c, 1, 1)
+                value = k[0] * c + k[1] * n + k[2] * s + k[3] * sides
+                dst[p - shift, block, :] = value.astype(dst.dtype)
+            return 0
+
+        lax.fori_loop(low, high, body, 0)
+
+    own_load.wait()
+
+    def early_at(g):
+        return halo * (1 - (g + groups - 1) // groups)
+
+    def late_at(g):
+        return (patch - halo) * ((g + groups - 1) // groups)
+
+    early = patch - halo
+
+    def interior(g):
+        low = g * patch + early_at(g) + halo
+        high = low + early
+        step(padded, first, 0, low - 2, high + 2)
+        step(first, second, 0, low - 1, high + 1)
+        step(second, fc, halo, low, high)
+
+    def edge(g):
+        inner = (g + groups - 1) // groups
+        end = g * patch + patch
+        for s, (src, dst, shift) in enumerate(((padded, first, 0), (first, second, 0), (second, fc, halo))):
+            low = (s - 2) * (1 - inner) + (end - 1 - s) * inner + halo
+            step(src, dst, shift, low, low + halo)
+
+    for j in range(1, groups):
+        interior(lax.rem(m + j, groups))
+
     pl.semaphore_wait(barrier, groups + 1)
 
     copies = []
@@ -80,54 +131,6 @@
         send(info_out, info_in.at[1], above),
     ]
 
-    def put_coef(base, d, a):
-        rows = pl.ds(base, d.shape[0])
-        coef[0, rows] = 1.0 - 4.0 * d
-        coef[1, rows] = d + 0.5 * a
-        coef[2, rows] = d - 0.5 * a
-        coef[3, rows] = d
-
-    put_coef(8, dif_ref[...], adv_ref[...])
-
-    def step(src, dst, shift, low, high):
-        def body(p, _):
-            k = [coef[i, pl.ds(p + 8 - halo, 1), :] for i in range(4)]
-            for at in range(0, local, MEMBER_BLOCK):
-                block = pl.ds(at, MEMBER_BLOCK)
-                c = src[p, block, :].astype(F32)
-                n = src[p - 1, block, :].astype(F32)
-                s = src[p + 1, block, :].astype(F32)
-                sides = pltpu.roll(c, width - 1, 1) + pltpu.roll(c, 1, 1)
-                value = k[0] * c + k[1] * n + k[2] * s + k[3] * sides
-                dst[p - shift, block, :] = value.astype(dst.dtype)
-            return 0
-
-        lax.fori_loop(low, high, body, 0)
-
-    own_load.wait()
-
-    def early_at(g):
-        return halo * (1 - (g + groups - 1) // groups)
-
-    def late_at(g):
-        return (patch - halo) * ((g + groups - 1) // groups)
-
-    early = patch - halo
-
-    def interior(g):
-        low = g * patch + early_at(g) + halo
-        high = low + early
-        step(padded, first, 0, low - 2, high + 2)
-        step(first, second, 0, low - 1, high + 1)
-        step(second, fc, halo, low, high)
-
-    def edge(g):
-        inner = (g + groups - 1) // groups
-        end = g * patch + patch
-        for s, (src, dst, shift) in enumerate(((padded, first, 0), (first, second, 0), (second, fc, halo))):
-            low = (s - 2) * (1 - inner) + (end - 1 - s) * inner + halo
-            step(src, dst, shift, low, low + halo)
-
     forwards = []
 
     def forward(j, late, at, count):
@@ -140,8 +143,8 @@
         )))
 
     for j in range(1, groups):
-        interior(lax.rem(m + j, groups))
-        forward(j, False, 0, early - 2)
+        forward(j, False, 0, early - 1)
+    interior(m)
 
     halo_top.wait_recv()
     halo_bottom.wait_recv()
@@ -164,9 +167,8 @@
         cell_copies[groups - j - 1].wait_recv()
         hsend[j - 1] = observe(g, cells_in[groups - j - 1, 0:1, :])
         hx.append(send(hsend.at[j - 1], hall.at[0, pl.ds(m * local, local)], (g, r)))
-        forward(j, False, early - 2, 1)
+        forward(j, False, early - 1, 1)
     own_rows = pl.ds(pl.multiple_of(m * local, local), local)
-    interior(m)
     edge(m)
     hall[0, own_rows, :] = observe(m, cell_ref[0])
 
@@ -183,7 +185,6 @@
     for j in range(1, groups):
         hx[j - 1].wait_recv()
         relays += relay(lax.rem(m + groups - j, groups))
-        forward(j, False, early - 1, 1)
         forward(j, True, 0, halo)
 
     row_id = lax.broadcasted_iota(jnp.int32, (members, members), 0)
@@ -212,7 +213,7 @@
             xbar[0:1, lane] = mean
             xb[:, lane] = (x - mean).astype(BF16)
 
-    for late, copy in forwards[:2 * (groups - 1)]:
+    for late, copy in forwards[:groups - 1]:
         copy.wait_recv()
     perturb(early_at(m), early - 1)
     for copy in info_copies + relays:
@@ -244,16 +245,19 @@
     def row_of(g, cut):
         return cut[1] + (late_at(g) if cut[0] else early_at(g))
 
+    def place(line, value):
+        out_ref[pl.ds(line, local, stride=lines), :] = value
+
     returns = []
     for cut in cuts:
         l, count = row_of(m, cut), cut[2]
         if cut[0]:
-            for late, copy in forwards[2 * (groups - 1):]:
+            for late, copy in forwards[groups - 1:]:
                 if late:
                     copy.wait_recv()
             perturb(late_at(m), halo)
         elif cut[1] == early - 1:
-            for late, copy in forwards[2 * (groups - 1):]:
+            for late, copy in forwards[groups - 1:]:
                 if not late:
                     copy.wait_recv()
             perturb(l, 1)
@@ -268,13 +272,13 @@
         l, count = row_of(m, cut), cut[2]
         value = result(m, l, count)
         for i in range(count):
-            out_ref[m * patch + l + i] = value[:, i * width:(i + 1) * width]
+            place(m * patch + l + i, value[:, i * width:(i + 1) * width])
     for j, cut, copy in returns:
         copy.wait_recv()
         g = lax.rem(m + groups - j, groups)
         l = row_of(g, cut)
         for i in range(cut[2]):
-            out_ref[g * patch + l + i] = ret_in[j - 1, l + i].astype(F32)
+            place(g * patch + l + i, ret_in[j - 1, l + i].astype(F32))
     for copy in copies:
         copy.wait_send()
 
@@ -285,12 +289,12 @@
     patch = lines // groups
     total = groups * local
     partners = groups - 1
-    count = 8 + partners + 4 * partners + partners + 2 * groups + 4 * partners
+    count = 8 + partners + 3 * partners + partners + 2 * groups + 4 * partners
     vmem = pl.BlockSpec(memory_space=pltpu.VMEM)
     flops = 2 * total * total * (3 * slots + 2 * total + patch * width)
     result = pl.pallas_call(
         functools.partial(kernel, groups, regions),
-        out_shape=jax.ShapeDtypeStruct((lines, local, width), F32),
+        out_shape=jax.ShapeDtypeStruct((local * lines, width), F32),
         in_specs=[pl.BlockSpec(memory_space=pl.ANY)] + [vmem] * 7,
         out_specs=vmem,
         scratch_shapes=[
@@ -324,7 +328,7 @@
         jnp.transpose(members, (1, 0, 2)), diffusivity, advection, obs_value, obs_rinv,
         obs_cell, obs_count, loc_index,
     )
-    return jnp.transpose(result, (1, 0, 2))
+    return result.reshape(local, lines, width)
 
 
 def solution(mesh):

time: 44.6 us -> 41.3 us (0.926)
  Pallas kernels: 39.6 us -> 37.5 us
  local copies, waits for them, and re-layouts: 4.06 us -> 2.84 us
    transpose x1 -> x0, local copies, waits for them, and re-layouts: 2.54 us -> none  [on_device(): return jnp.transpose(result, (1, 0, 2))]
    pallas_call x1, Pallas kernels: 39.6 us -> 37.5 us  [on_device(): pl.pallas_call(functools.partial(kernel, groups, regions), out_shape=jax....]
    unnamed x13 -> x14, local copies, waits for them, and re-layouts: 1.52 us -> 2.84 us
where the time goes in v3:
time: 41.3 us; the launch traced here: 41.1 us
  Pallas kernels  37.5 us (91%)
  local copies, waits for them, and re-layouts  2.84 us (7%)
  between operations  0.8 us (2%)
    pallas_call x1, Pallas kernels, on_device(): pl.pallas_call(functools.partial(kernel, groups, regions), out_shape=jax....  37.5 us
    unnamed x14, local copies, waits for them, and re-layouts  2.84 us

profile of v3, /device:TPU:0, one launch (start us, length us, event | category | flops | bytes accessed | tf_op | source)
XLA Modules:
  0.0 41.1 jit_solution(3409390261772745589)
XLA Ops:
  0.0 0.0 copy-start.5
  0.0 0.0 copy-start.4
  0.0 0.0 copy-start.3
  0.0 0.0 copy-start.2
  0.0 0.0 copy-start.1
  0.0 0.0 copy-start
  0.7 1.5 %copy.11 = bf16[256,16,128]{2,0,1:T(8,128)(2,1)S(1)} copy(bf16[256,16,128]{2,1,0:T(8,128)(2,1)} %param.8) | data formatting | bytes 2097152 | tf_op args[0]
  2.2 0.0 copy-done.5
  2.3 0.0 copy-done.4
  2.3 0.0 copy-done.3
  2.3 0.0 copy-done.2
  2.3 0.0 copy-done.1
  2.3 0.0 copy-done
  2.3 37.5 %shard_map.82 = f32[4096,128]{1,0:T(8,128)S(1)} custom-call(bf16[16,256,128]{2,1,0:T(8,128)(2,1)S(1)} %bitcast.5, f32[16,128]{1,0:T(8,128)S(1)} %copy-done, f32[16,128]{1,0:T(8,128)S(1)} %copy-done.1, bf16[1,1,256]{2,1,0:T(2,128)(2,1)S(1)} %copy-done.2, f32[1,1,256]{2,1,0:T(1,128)S(1)} %copy-done.3, s32[1,1,256]{2,1,0:T(1,128)S(1)} %copy-done.4, ...), custom_call_target="tpu_custom_call" | custom-call | flops 1476395008 | bytes 3145728 | tf_op jit(solution)/shard_map/pallas_call | solution.py:295
  39.8 1.3 %copy.14 = f32[256,16,128]{2,1,0:T(8,128)} copy(f32[256,16,128]{2,1,0:T(8,128)S(1)} %bitcast.4) | data formatting | bytes 4194304
Async XLA Ops:
  0.0 2.2 %copy-start.5 = (s32[1,1,256]{2,1,0:T(1,128)S(1)}, s32[1,1,256]{2,1,0:T(1,128)}, u32[]{:S(2)}) copy-start(s32[1,1,256]{2,1,0:T(1,128)} %loc_ref.1) | copy-start | bytes 3076
  0.0 2.3 %copy-start.4 = (s32[1,1,256]{2,1,0:T(1,128)S(1)}, s32[1,1,256]{2,1,0:T(1,128)}, u32[]{:S(2)}) copy-start(s32[1,1,256]{2,1,0:T(1,128)} %cell_ref.1) | copy-start | bytes 3076
  0.0 2.3 %copy-start.3 = (f32[1,1,256]{2,1,0:T(1,128)S(1)}, f32[1,1,256]{2,1,0:T(1,128)}, u32[]{:S(2)}) copy-start(f32[1,1,256]{2,1,0:T(1,128)} %rinv_ref.1) | copy-start | bytes 3076
  0.0 2.3 %copy-start.2 = (bf16[1,1,256]{2,1,0:T(2,128)(2,1)S(1)}, bf16[1,1,256]{2,1,0:T(2,128)(2,1)}, u32[]{:S(2)}) copy-start(bf16[1,1,256]{2,1,0:T(2,128)(2,1)} %val_ref.1) | copy-start | bytes 1540
  0.0 2.3 %copy-start.1 = (f32[16,128]{1,0:T(8,128)S(1)}, f32[16,128]{1,0:T(8,128)}, u32[]{:S(2)}) copy-start(f32[16,128]{1,0:T(8,128)} %adv_ref.1) | copy-start | bytes 24580
  0.0 2.3 %copy-start = (f32[16,128]{1,0:T(8,128)S(1)}, f32[16,128]{1,0:T(8,128)}, u32[]{:S(2)}) copy-start(f32[16,128]{1,0:T(8,128)} %dif_ref.1) | copy-start | bytes 24580

commit v4 on v3

--- a/solution.py
+++ b/solution.py
@@ -143,7 +143,7 @@
         )))
 
     for j in range(1, groups):
-        forward(j, False, 0, early - 1)
+        forward(j, False, 0, early - 2)
     interior(m)
 
     halo_top.wait_recv()
@@ -160,31 +160,36 @@
         pick = jnp.where(cell_index == cells, 1.0, 0.0).astype(BF16)
         return jnp.dot(flat, pick, preferred_element_type=F32).astype(BF16)
 
+    half_rows = local // 2
     hx = []
     for j in range(1, groups):
         g = lax.rem(m + j, groups)
         edge(g)
         cell_copies[groups - j - 1].wait_recv()
         hsend[j - 1] = observe(g, cells_in[groups - j - 1, 0:1, :])
-        hx.append(send(hsend.at[j - 1], hall.at[0, pl.ds(m * local, local)], (g, r)))
-        forward(j, False, early - 1, 1)
+        for at in range(0, local, half_rows):
+            hx.append((j, at, send(
+                hsend.at[j - 1, pl.ds(at, half_rows)], hall.at[0, pl.ds(m * local + at, half_rows)], (g, r)
+            )))
+        forward(j, False, early - 2, 2)
     own_rows = pl.ds(pl.multiple_of(m * local, local), local)
     edge(m)
     hall[0, own_rows, :] = observe(m, cell_ref[0])
 
-    def relay(block):
-        rows = pl.ds(block * local, local)
+    def relay(start, count):
+        rows = pl.ds(start, count)
         return [
             send(hall.at[0, rows], hall.at[1, rows], below),
             send(hall.at[0, rows], hall.at[2, rows], above),
         ]
 
-    relays = relay(m)
+    relays = relay(m * local, local)
     for l in range(patch):
         states[l, own_rows, :] = fc[m * patch + l]
-    for j in range(1, groups):
-        hx[j - 1].wait_recv()
-        relays += relay(lax.rem(m + groups - j, groups))
+    for j, at, copy in hx:
+        copy.wait_recv()
+        relays += relay(lax.rem(m + groups - j, groups) * local + at, half_rows)
+    for j in range(1, groups):
         forward(j, True, 0, halo)
 
     row_id = lax.broadcasted_iota(jnp.int32, (members, members), 0)
@@ -215,10 +220,10 @@
 
     for late, copy in forwards[:groups - 1]:
         copy.wait_recv()
-    perturb(early_at(m), early - 1)
-    for copy in info_copies + relays:
-        copy.wait_recv()
+    perturb(early_at(m), early - 2)
     for side in range(2):
+        for copy in [info_copies[side]] + relays[side::2]:
+            copy.wait_recv()
         part, more = gram(hall[1 + side], info_in[side, 0:1, :], info_in[side, 1:2, :])
         system, force = system + part, force + more
     total = jnp.sum(jnp.sum(system * system, axis=0, keepdims=True), axis=1, keepdims=True)
@@ -240,7 +245,7 @@
         rows = pl.ds(pl.multiple_of(g * local, local), local)
         return xbar[0:1, lane] + jnp.dot(wt[rows, :], xb[:, lane], preferred_element_type=F32)
 
-    cuts = ((False, 0, early - 3), (False, early - 3, 2), (False, early - 1, 1), (True, 0, halo))
+    cuts = ((False, 0, early - 2), (False, early - 2, 2), (True, 0, halo - 1), (True, halo - 1, 1))
 
     def row_of(g, cut):
         return cut[1] + (late_at(g) if cut[0] else early_at(g))
@@ -251,16 +256,16 @@
     returns = []
     for cut in cuts:
         l, count = row_of(m, cut), cut[2]
-        if cut[0]:
+        if cut == cuts[1]:
+            for late, copy in forwards[groups - 1:]:
+                if not late:
+                    copy.wait_recv()
+            perturb(l, count)
+        elif cut == cuts[2]:
             for late, copy in forwards[groups - 1:]:
                 if late:
                     copy.wait_recv()
             perturb(late_at(m), halo)
-        elif cut[1] == early - 1:
-            for late, copy in forwards[groups - 1:]:
-                if not late:
-                    copy.wait_recv()
-            perturb(l, 1)
         for j in range(1, groups):
             g = lax.rem(m + j, groups)
             value = result(g, l, count).astype(BF16)
@@ -289,7 +294,7 @@
     patch = lines // groups
     total = groups * local
     partners = groups - 1
-    count = 8 + partners + 3 * partners + partners + 2 * groups + 4 * partners
+    count = 8 + partners + 3 * partners + 2 * partners + 2 + 4 * partners + 4 * partners
     vmem = pl.BlockSpec(memory_space=pltpu.VMEM)
     flops = 2 * total * total * (3 * slots + 2 * total + patch * width)
     result = pl.pallas_call(

time: 41.3 us -> 41.9 us (1.015)
  Pallas kernels: 37.5 us -> 38.1 us
    pallas_call x1, Pallas kernels: 37.5 us -> 38.1 us  [on_device(): pl.pallas_call(functools.partial(kernel, groups, regions), out_shape=jax....]
where the time goes in v4:
time: 41.9 us; the launch traced here: 41.7 us
  Pallas kernels  38.1 us (91%)
  local copies, waits for them, and re-layouts  2.84 us (7%)
  between operations  0.8 us (2%)
    pallas_call x1, Pallas kernels, on_device(): pl.pallas_call(functools.partial(kernel, groups, regions), out_shape=jax....  38.1 us
    unnamed x14, local copies, waits for them, and re-layouts  2.84 us

profile of v4, /device:TPU:0, one launch (start us, length us, event | category | flops | bytes accessed | tf_op | source)
XLA Modules:
  0.0 41.7 jit_solution(16078017459190955666)
XLA Ops:
  0.0 0.0 copy-start.5
  0.0 0.0 copy-start.4
  0.0 0.0 copy-start.3
  0.0 0.0 copy-start.2
  0.0 0.0 copy-start.1
  0.0 0.0 copy-start
  0.7 1.5 %copy.11 = bf16[256,16,128]{2,0,1:T(8,128)(2,1)S(1)} copy(bf16[256,16,128]{2,1,0:T(8,128)(2,1)} %param.8) | data formatting | bytes 2097152 | tf_op args[0]
  2.2 0.0 copy-done.5
  2.3 0.0 copy-done.4
  2.3 0.0 copy-done.3
  2.3 0.0 copy-done.2
  2.3 0.0 copy-done.1
  2.3 0.0 copy-done
  2.3 38.1 %shard_map.82 = f32[4096,128]{1,0:T(8,128)S(1)} custom-call(bf16[16,256,128]{2,1,0:T(8,128)(2,1)S(1)} %bitcast.5, f32[16,128]{1,0:T(8,128)S(1)} %copy-done, f32[16,128]{1,0:T(8,128)S(1)} %copy-done.1, bf16[1,1,256]{2,1,0:T(2,128)(2,1)S(1)} %copy-done.2, f32[1,1,256]{2,1,0:T(1,128)S(1)} %copy-done.3, s32[1,1,256]{2,1,0:T(1,128)S(1)} %copy-done.4, ...), custom_call_target="tpu_custom_call" | custom-call | flops 1476395008 | bytes 3145728 | tf_op jit(solution)/shard_map/pallas_call | solution.py:300
  40.4 1.3 %copy.14 = f32[256,16,128]{2,1,0:T(8,128)} copy(f32[256,16,128]{2,1,0:T(8,128)S(1)} %bitcast.4) | data formatting | bytes 4194304
Async XLA Ops:
  0.0 2.2 %copy-start.5 = (s32[1,1,256]{2,1,0:T(1,128)S(1)}, s32[1,1,256]{2,1,0:T(1,128)}, u32[]{:S(2)}) copy-start(s32[1,1,256]{2,1,0:T(1,128)} %loc_ref.1) | copy-start | bytes 3076
  0.0 2.3 %copy-start.4 = (s32[1,1,256]{2,1,0:T(1,128)S(1)}, s32[1,1,256]{2,1,0:T(1,128)}, u32[]{:S(2)}) copy-start(s32[1,1,256]{2,1,0:T(1,128)} %cell_ref.1) | copy-start | bytes 3076
  0.0 2.3 %copy-start.3 = (f32[1,1,256]{2,1,0:T(1,128)S(1)}, f32[1,1,256]{2,1,0:T(1,128)}, u32[]{:S(2)}) copy-start(f32[1,1,256]{2,1,0:T(1,128)} %rinv_ref.1) | copy-start | bytes 3076
  0.0 2.3 %copy-start.2 = (bf16[1,1,256]{2,1,0:T(2,128)(2,1)S(1)}, bf16[1,1,256]{2,1,0:T(2,128)(2,1)}, u32[]{:S(2)}) copy-start(bf16[1,1,256]{2,1,0:T(2,128)(2,1)} %val_ref.1) | copy-start | bytes 1540
  0.0 2.3 %copy-start.1 = (f32[16,128]{1,0:T(8,128)S(1)}, f32[16,128]{1,0:T(8,128)}, u32[]{:S(2)}) copy-start(f32[16,128]{1,0:T(8,128)} %adv_ref.1) | copy-start | bytes 24580
  0.0 2.3 %copy-start = (f32[16,128]{1,0:T(8,128)S(1)}, f32[16,128]{1,0:T(8,128)}, u32[]{:S(2)}) copy-start(f32[16,128]{1,0:T(8,128)} %dif_ref.1) | copy-start | bytes 24580

commit v5 on v3

--- a/solution.py
+++ b/solution.py
@@ -81,10 +81,13 @@
 
     early = patch - halo
 
-    def interior(g):
+    def interior_first(g):
+        low = g * patch + early_at(g) + halo
+        step(padded, first, 0, low - 2, low + early + 2)
+
+    def interior_rest(g):
         low = g * patch + early_at(g) + halo
         high = low + early
-        step(padded, first, 0, low - 2, high + 2)
         step(first, second, 0, low - 1, high + 1)
         step(second, fc, halo, low, high)
 
@@ -96,7 +99,7 @@
             step(src, dst, shift, low, low + halo)
 
     for j in range(1, groups):
-        interior(lax.rem(m + j, groups))
+        interior_first(lax.rem(m + j, groups))
 
     pl.semaphore_wait(barrier, groups + 1)
 
@@ -143,8 +146,10 @@
         )))
 
     for j in range(1, groups):
+        interior_rest(lax.rem(m + j, groups))
         forward(j, False, 0, early - 1)
-    interior(m)
+    interior_first(m)
+    interior_rest(m)
 
     halo_top.wait_recv()
     halo_bottom.wait_recv()

time: 41.3 us -> 42.3 us (1.024)
  Pallas kernels: 37.5 us -> 38.5 us
    pallas_call x1, Pallas kernels: 37.5 us -> 38.5 us  [on_device(): pl.pallas_call(functools.partial(kernel, groups, regions), out_shape=jax....]
where the time goes in v5:
time: 42.3 us; the launch traced here: 42.1 us
  Pallas kernels  38.5 us (91%)
  local copies, waits for them, and re-layouts  2.84 us (7%)
  between operations  0.8 us (2%)
    pallas_call x1, Pallas kernels, on_device(): pl.pallas_call(functools.partial(kernel, groups, regions), out_shape=jax....  38.5 us
    unnamed x14, local copies, waits for them, and re-layouts  2.84 us

profile of v5, /device:TPU:0, one launch (start us, length us, event | category | flops | bytes accessed | tf_op | source)
XLA Modules:
  0.0 42.1 jit_solution(2325433321582528527)
XLA Ops:
  0.0 0.0 copy-start.5
  0.0 0.0 copy-start.4
  0.0 0.0 copy-start.3
  0.0 0.0 copy-start.2
  0.0 0.0 copy-start.1
  0.0 0.0 copy-start
  0.7 1.5 %copy.11 = bf16[256,16,128]{2,0,1:T(8,128)(2,1)S(1)} copy(bf16[256,16,128]{2,1,0:T(8,128)(2,1)} %param.8) | data formatting | bytes 2097152 | tf_op args[0]
  2.2 0.0 copy-done.5
  2.3 0.0 copy-done.4
  2.3 0.0 copy-done.3
  2.3 0.0 copy-done.2
  2.3 0.0 copy-done.1
  2.3 0.0 copy-done
  2.3 38.5 %shard_map.82 = f32[4096,128]{1,0:T(8,128)S(1)} custom-call(bf16[16,256,128]{2,1,0:T(8,128)(2,1)S(1)} %bitcast.5, f32[16,128]{1,0:T(8,128)S(1)} %copy-done, f32[16,128]{1,0:T(8,128)S(1)} %copy-done.1, bf16[1,1,256]{2,1,0:T(2,128)(2,1)S(1)} %copy-done.2, f32[1,1,256]{2,1,0:T(1,128)S(1)} %copy-done.3, s32[1,1,256]{2,1,0:T(1,128)S(1)} %copy-done.4, ...), custom_call_target="tpu_custom_call" | custom-call | flops 1476395008 | bytes 3145728 | tf_op jit(solution)/shard_map/pallas_call | solution.py:300
  40.8 1.3 %copy.14 = f32[256,16,128]{2,1,0:T(8,128)} copy(f32[256,16,128]{2,1,0:T(8,128)S(1)} %bitcast.4) | data formatting | bytes 4194304
Async XLA Ops:
  0.0 2.2 %copy-start.5 = (s32[1,1,256]{2,1,0:T(1,128)S(1)}, s32[1,1,256]{2,1,0:T(1,128)}, u32[]{:S(2)}) copy-start(s32[1,1,256]{2,1,0:T(1,128)} %loc_ref.1) | copy-start | bytes 3076
  0.0 2.3 %copy-start.4 = (s32[1,1,256]{2,1,0:T(1,128)S(1)}, s32[1,1,256]{2,1,0:T(1,128)}, u32[]{:S(2)}) copy-start(s32[1,1,256]{2,1,0:T(1,128)} %cell_ref.1) | copy-start | bytes 3076
  0.0 2.3 %copy-start.3 = (f32[1,1,256]{2,1,0:T(1,128)S(1)}, f32[1,1,256]{2,1,0:T(1,128)}, u32[]{:S(2)}) copy-start(f32[1,1,256]{2,1,0:T(1,128)} %rinv_ref.1) | copy-start | bytes 3076
  0.0 2.3 %copy-start.2 = (bf16[1,1,256]{2,1,0:T(2,128)(2,1)S(1)}, bf16[1,1,256]{2,1,0:T(2,128)(2,1)}, u32[]{:S(2)}) copy-start(bf16[1,1,256]{2,1,0:T(2,128)(2,1)} %val_ref.1) | copy-start | bytes 1540
  0.0 2.3 %copy-start.1 = (f32[16,128]{1,0:T(8,128)S(1)}, f32[16,128]{1,0:T(8,128)}, u32[]{:S(2)}) copy-start(f32[16,128]{1,0:T(8,128)} %adv_ref.1) | copy-start | bytes 24580
  0.0 2.3 %copy-start = (f32[16,128]{1,0:T(8,128)S(1)}, f32[16,128]{1,0:T(8,128)}, u32[]{:S(2)}) copy-start(f32[16,128]{1,0:T(8,128)} %dif_ref.1) | copy-start | bytes 24580

commit v6 on v3

--- a/solution.py
+++ b/solution.py
@@ -216,9 +216,9 @@
     for late, copy in forwards[:groups - 1]:
         copy.wait_recv()
     perturb(early_at(m), early - 1)
-    for copy in info_copies + relays:
-        copy.wait_recv()
     for side in range(2):
+        for copy in [info_copies[side]] + relays[side::2]:
+            copy.wait_recv()
         part, more = gram(hall[1 + side], info_in[side, 0:1, :], info_in[side, 1:2, :])
         system, force = system + part, force + more
     total = jnp.sum(jnp.sum(system * system, axis=0, keepdims=True), axis=1, keepdims=True)

time: 41.3 us -> 41.9 us (1.015)
  Pallas kernels: 37.5 us -> 38.1 us
    pallas_call x1, Pallas kernels: 37.5 us -> 38.1 us  [on_device(): pl.pallas_call(functools.partial(kernel, groups, regions), out_shape=jax....]
where the time goes in v6:
time: 41.9 us; the launch traced here: 41.8 us
  Pallas kernels  38.1 us (91%)
  local copies, waits for them, and re-layouts  2.84 us (7%)
  between operations  0.8 us (2%)
    pallas_call x1, Pallas kernels, on_device(): pl.pallas_call(functools.partial(kernel, groups, regions), out_shape=jax....  38.1 us
    unnamed x14, local copies, waits for them, and re-layouts  2.84 us

profile of v6, /device:TPU:0, one launch (start us, length us, event | category | flops | bytes accessed | tf_op | source)
XLA Modules:
  0.0 41.8 jit_solution(5478817925791218116)
XLA Ops:
  0.0 0.0 copy-start.5
  0.0 0.0 copy-start.4
  0.0 0.0 copy-start.3
  0.0 0.0 copy-start.2
  0.0 0.0 copy-start.1
  0.0 0.0 copy-start
  0.7 1.5 %copy.11 = bf16[256,16,128]{2,0,1:T(8,128)(2,1)S(1)} copy(bf16[256,16,128]{2,1,0:T(8,128)(2,1)} %param.8) | data formatting | bytes 2097152 | tf_op args[0]
  2.2 0.0 copy-done.5
  2.3 0.0 copy-done.4
  2.3 0.0 copy-done.3
  2.3 0.0 copy-done.2
  2.3 0.0 copy-done.1
  2.3 0.0 copy-done
  2.3 38.1 %shard_map.82 = f32[4096,128]{1,0:T(8,128)S(1)} custom-call(bf16[16,256,128]{2,1,0:T(8,128)(2,1)S(1)} %bitcast.5, f32[16,128]{1,0:T(8,128)S(1)} %copy-done, f32[16,128]{1,0:T(8,128)S(1)} %copy-done.1, bf16[1,1,256]{2,1,0:T(2,128)(2,1)S(1)} %copy-done.2, f32[1,1,256]{2,1,0:T(1,128)S(1)} %copy-done.3, s32[1,1,256]{2,1,0:T(1,128)S(1)} %copy-done.4, ...), custom_call_target="tpu_custom_call" | custom-call | flops 1476395008 | bytes 3145728 | tf_op jit(solution)/shard_map/pallas_call | solution.py:295
  40.4 1.3 %copy.14 = f32[256,16,128]{2,1,0:T(8,128)} copy(f32[256,16,128]{2,1,0:T(8,128)S(1)} %bitcast.4) | data formatting | bytes 4194304
Async XLA Ops:
  0.0 2.2 %copy-start.5 = (s32[1,1,256]{2,1,0:T(1,128)S(1)}, s32[1,1,256]{2,1,0:T(1,128)}, u32[]{:S(2)}) copy-start(s32[1,1,256]{2,1,0:T(1,128)} %loc_ref.1) | copy-start | bytes 3076
  0.0 2.3 %copy-start.4 = (s32[1,1,256]{2,1,0:T(1,128)S(1)}, s32[1,1,256]{2,1,0:T(1,128)}, u32[]{:S(2)}) copy-start(s32[1,1,256]{2,1,0:T(1,128)} %cell_ref.1) | copy-start | bytes 3076
  0.0 2.3 %copy-start.3 = (f32[1,1,256]{2,1,0:T(1,128)S(1)}, f32[1,1,256]{2,1,0:T(1,128)}, u32[]{:S(2)}) copy-start(f32[1,1,256]{2,1,0:T(1,128)} %rinv_ref.1) | copy-start | bytes 3076
  0.0 2.3 %copy-start.2 = (bf16[1,1,256]{2,1,0:T(2,128)(2,1)S(1)}, bf16[1,1,256]{2,1,0:T(2,128)(2,1)}, u32[]{:S(2)}) copy-start(bf16[1,1,256]{2,1,0:T(2,128)(2,1)} %val_ref.1) | copy-start | bytes 1540
  0.0 2.3 %copy-start.1 = (f32[16,128]{1,0:T(8,128)S(1)}, f32[16,128]{1,0:T(8,128)}, u32[]{:S(2)}) copy-start(f32[16,128]{1,0:T(8,128)} %adv_ref.1) | copy-start | bytes 24580
  0.0 2.3 %copy-start = (f32[16,128]{1,0:T(8,128)S(1)}, f32[16,128]{1,0:T(8,128)}, u32[]{:S(2)}) copy-start(f32[16,128]{1,0:T(8,128)} %dif_ref.1) | copy-start | bytes 24580
